TPU v7x, 32 devices: a whole 2x2x4 slice. The times are simulated.
32 devices in a mesh: groups: 2 (over y), ctx: 4 (over z), tp: 4 (over x, core).
Axes of the slice: x: 2, y: 2, z: 4, core: 2. Of those that a mesh axis runs over, the one named last changes fastest.
Arguments:
- hidden: bfloat16 [1024, 8192], P(('groups', 'ctx'), 'tp'), parts along dimension 0, may hold values from -6 to 6
- base_query_rows: bfloat16 [1024, 8192], P(('groups', 'ctx'), 'tp'), parts along dimension 0, may hold values from -60 to 60
- base_key_rows: bfloat16 [1024, 1024], P(('groups', 'ctx'), 'tp'), parts along dimension 0, may hold values from -60 to 60
- base_value_rows: bfloat16 [1024, 1024], P(('groups', 'ctx'), 'tp'), parts along dimension 0, may hold values from -6 to 6
- stored_block_order: int32 [16], P('groups'), parts along dimension 0, may hold values from 0 to 7, each once
- version: int32 [8], P('groups'), parts along dimension 0, may hold values from 0 to 3
- publisher: int32 [2], P('groups'), parts along dimension 0, may hold values from 0 to 3
- adapter_down_weight: bfloat16 [4, 4, 192, 8192], P('ctx', None, None, 'tp'), may hold values from -0.0625 to 0.0625
- adapter_up_query: bfloat16 [4, 4, 64, 8192], P('ctx', None, None, 'tp'), may hold values from -0.75 to 0.75
- adapter_up_key_value: bfloat16 [4, 4, 2, 64, 1024], P('ctx', None, None, None, 'tp'), may hold values from -0.75 to 0.75
- output_down_weight: bfloat16 [4, 4, 64, 8192], P('ctx', None, None, 'tp'), may hold values from -0.1875 to 0.1875
- output_up_weight: bfloat16 [4, 4, 64, 8192], P('ctx', None, None, 'tp'), may hold values from -0.75 to 0.75
Outputs:
- attended: bfloat16 [1024, 8192], P(('groups', 'ctx'), 'tp'), parts along dimension 0
- adapted: bfloat16 [1024, 8192], P(('groups', 'ctx'), 'tp'), parts along dimension 0
There are 2 independent parts, one for each index of `groups`. A program takes and returns all parts, laid end to end along the dimension named above; an argument that names none is the same for every part. Nothing has to cross between parts.
Inputs may be any that keep to these rules, and one draw needn't show every extreme that they name: `stored_block_order`: each half-block of the prompt is stored exactly once.
All inputs are finite; a program needn't handle non-finite values.
Results may differ from a plain program's by a relative error of at most 0.015.
The roundings to bfloat16 on the way count: a program that leaves them out, or rounds other values in their place, can miss the bound.
Values may be sent and summed in bfloat16 or wider, within the bound.
A program may use at most 64 MiB of HBM per device.

v0:
```python
import jax
import jax.numpy as jnp
from jax import lax
from jax.sharding import PartitionSpec as P

HEAD_SIZE = 128
ADAPTER_RANK = 64


NEG_BIG = -1e30


def spread(value, axis, source):
    kept = jnp.where(lax.axis_index(axis) == source, value, 0).astype(value.dtype)
    return lax.psum(kept, axis)


def from_behind(value, axis, steps):
    count = lax.axis_size(axis)
    pairs = [(source, (source + steps) % count) for source in range(count)]
    return lax.ppermute(value, axis, pairs)


def apply_rotation(values, token_index_list):
    half_dim = values.shape[-1] // 2
    frequency = 500000.0 ** (-(jnp.arange(half_dim, dtype=jnp.float32) * 2.0) / values.shape[-1])
    angles = token_index_list.astype(jnp.float32)[:, None] * frequency[None, :]
    cosine = jnp.cos(angles)[:, None, :]
    sine_part = jnp.sin(angles)[:, None, :]
    first_half = values[..., :half_dim]
    second_half = values[..., half_dim:]
    return jnp.concatenate(
        [
            first_half * cosine - second_half * sine_part,
            second_half * cosine + first_half * sine_part,
        ],
        axis=-1,
    )


def pick_slot_version(stored, chosen_version):
    return lax.dynamic_index_in_dim(stored[0], chosen_version, 0, keepdims=False)


def token_positions(stored_block_order, first_row, row_count, half_rows):
    flat_index = first_row + jnp.arange(row_count, dtype=jnp.int32)
    block_index = flat_index // half_rows
    matches = (
        block_index[:, None] == jnp.arange(stored_block_order.shape[0], dtype=jnp.int32)[None, :]
    )
    stored_block = jnp.sum(jnp.where(matches, stored_block_order[None, :], 0), axis=1)
    return stored_block * half_rows + flat_index % half_rows


def attend_block(
    softmax_state, adapted_queries, query_pos, adapted_key_rows, adapted_value_rows, key_pos
):
    running_max, totals, accum = softmax_state
    scores = jnp.einsum(
        "tkgd,skd->kgts", adapted_queries, adapted_key_rows, preferred_element_type=jnp.float32
    ) * HEAD_SIZE ** (-0.5)
    visible = (key_pos[None, :] <= query_pos[:, None])[None, None]
    scores = jnp.where(visible, scores, NEG_BIG)
    new_max = jnp.maximum(running_max, jnp.max(scores, axis=-1))
    rescale = jnp.exp(running_max - new_max)
    raw_scores = jnp.where(visible, jnp.exp(scores - new_max[..., None]), 0.0)
    totals = totals * rescale + jnp.sum(raw_scores, axis=-1)
    accum = accum * rescale[..., None] + jnp.einsum(
        "kgts,skd->kgtd",
        raw_scores.astype(jnp.bfloat16),
        adapted_value_rows,
        preferred_element_type=jnp.float32,
    )
    return (new_max, totals, accum)


def shards(
    hidden,
    base_query_rows,
    base_key_rows,
    base_value_rows,
    stored_block_order,
    version,
    publisher,
    adapter_down_weight,
    adapter_up_query,
    adapter_up_key_value,
    output_down_weight,
    output_up_weight,
):
    source_block = publisher[0]
    chosen_version = lax.dynamic_index_in_dim(version, source_block, 0, keepdims=False)
    down_output, up_query, up_pair, outer_down, outer_up = (
        spread(pick_slot_version(adapter_down_weight, chosen_version), "ctx", source_block),
        spread(pick_slot_version(adapter_up_query, chosen_version), "ctx", source_block),
        spread(pick_slot_version(adapter_up_key_value, chosen_version), "ctx", source_block),
        spread(pick_slot_version(output_down_weight, chosen_version), "ctx", source_block),
        spread(pick_slot_version(output_up_weight, chosen_version), "ctx", source_block),
    )
    partial_value = lax.dot_general(
        hidden, down_output, (((1,), (1,)), ((), ())), preferred_element_type=jnp.float32
    )
    rank_projection = lax.psum(partial_value, "tp").astype(jnp.bfloat16)
    local_rows = hidden.shape[0]
    half_rows = local_rows // 2
    cycle_size = lax.axis_size("ctx")
    own_index = lax.axis_index("ctx")
    query_pos = token_positions(stored_block_order, own_index * local_rows, local_rows, half_rows)
    local_heads = base_query_rows.shape[1] // HEAD_SIZE
    local_groups = base_key_rows.shape[1] // HEAD_SIZE
    query_group_size = local_heads // local_groups
    adapted_queries = base_query_rows.astype(jnp.float32) + jnp.dot(
        rank_projection[:, :ADAPTER_RANK], up_query, preferred_element_type=jnp.float32
    )
    adapted_queries = apply_rotation(
        adapted_queries.reshape(local_rows, local_heads, HEAD_SIZE), query_pos
    ).astype(jnp.bfloat16)
    adapted_queries = adapted_queries.reshape(local_rows, local_groups, query_group_size, HEAD_SIZE)
    adapted_key_rows = base_key_rows.astype(jnp.float32) + jnp.dot(
        rank_projection[:, ADAPTER_RANK : 2 * ADAPTER_RANK],
        up_pair[0],
        preferred_element_type=jnp.float32,
    )
    adapted_key_rows = apply_rotation(
        adapted_key_rows.reshape(local_rows, local_groups, HEAD_SIZE), query_pos
    ).astype(jnp.bfloat16)
    adapted_value_rows = base_value_rows.astype(jnp.float32) + jnp.dot(
        rank_projection[:, 2 * ADAPTER_RANK :], up_pair[1], preferred_element_type=jnp.float32
    )
    adapted_value_rows = adapted_value_rows.astype(jnp.bfloat16).reshape(
        local_rows, local_groups, HEAD_SIZE
    )
    empty_state = (
        jnp.full((local_groups, query_group_size, local_rows), NEG_BIG, jnp.float32),
        jnp.zeros((local_groups, query_group_size, local_rows), jnp.float32),
        jnp.zeros((local_groups, query_group_size, local_rows, HEAD_SIZE), jnp.float32),
    )
    first_state = attend_block(
        empty_state, adapted_queries, query_pos, adapted_key_rows, adapted_value_rows, query_pos
    )

    def cycle_turn(turn, carried):
        moving_keys, moving_values, softmax_state = carried
        moving_keys, moving_values = from_behind((moving_keys, moving_values), "ctx", 1)
        sender = (own_index - turn - 1) % cycle_size
        key_pos = token_positions(stored_block_order, sender * local_rows, local_rows, half_rows)
        return (
            moving_keys,
            moving_values,
            attend_block(
                softmax_state, adapted_queries, query_pos, moving_keys, moving_values, key_pos
            ),
        )

    final_state = lax.fori_loop(
        0, cycle_size - 1, cycle_turn, (adapted_key_rows, adapted_value_rows, first_state)
    )[2]
    running_max, totals, accum = final_state
    attended = (
        jnp.transpose(accum / totals[..., None], (2, 0, 1, 3))
        .reshape(local_rows, local_heads * HEAD_SIZE)
        .astype(jnp.bfloat16)
    )
    out_partial = lax.dot_general(
        attended, outer_down, (((1,), (1,)), ((), ())), preferred_element_type=jnp.float32
    )
    out_low = lax.psum(out_partial.astype(jnp.bfloat16), "tp")
    adapted = jnp.dot(out_low, outer_up, preferred_element_type=jnp.float32).astype(jnp.bfloat16)
    return (attended, adapted)


def solution(mesh):
    placed = (
        P(("groups", "ctx"), "tp"),
        P(("groups", "ctx"), "tp"),
        P(("groups", "ctx"), "tp"),
        P(("groups", "ctx"), "tp"),
        P("groups"),
        P("groups"),
        P("groups"),
        P("ctx", None, None, "tp"),
        P("ctx", None, None, "tp"),
        P("ctx", None, None, None, "tp"),
        P("ctx", None, None, "tp"),
        P("ctx", None, None, "tp"),
    )
    return jax.shard_map(
        shards,
        mesh=mesh,
        in_specs=placed,
        out_specs=(P(("groups", "ctx"), "tp"), P(("groups", "ctx"), "tp")),
        check_vma=False,
    )
```

profile of v0, /device:TPU:0, one launch (start us, length us, event | category | flops | bytes accessed | tf_op | source)
XLA Modules:
  0.0 155.3 jit_solution(17024715240164693517)
XLA Ops:
  7.2 0.0 copy-start
  7.2 0.0 all-reduce.3.cloned.1.call-start
  7.9 1.2 dynamic_slice.22
  11.1 2.1 %select_bitcast_fusion = bf16[192,2048]{1,0:T(8,128)(2,1)} fusion(bf16[1,4,192,2048]{3,2,1,0:T(8,128)(2,1)} %param.21, s32[]{:T(128)S(6)} %select_n.191, pred[]{:T(512)S(6)} %eq.79), kind=kLoop, calls=%fused_computation.43 | loop fusion | flops 393216 | bytes 1572869 | tf_op jit(solution)/shard_map/jit(_where)/select_n | solution.py:14
  13.3 1.7 %select_bitcast_fusion.3 = bf16[64,2048]{1,0:T(8,128)(2,1)} fusion(bf16[1,4,64,2048]{3,2,1,0:T(8,128)(2,1)} %param.22, s32[]{:T(128)S(6)} %select_n.191, pred[]{:T(512)S(6)} %eq.79), kind=kLoop, calls=%fused_computation.52 | loop fusion | flops 131072 | bytes 524293 | tf_op jit(solution)/shard_map/jit(_where)/select_n | solution.py:14
  15.0 1.5 select_bitcast_fusion.4
  16.5 1.9 %select_bitcast_fusion.1 = (bf16[64,2048]{1,0:T(8,128)(2,1)}, bf16[64,2048]{1,0:T(8,128)(2,1)}) fusion(bf16[1,4,64,2048]{3,2,1,0:T(8,128)(2,1)} %param.25, s32[]{:T(128)S(6)} %select_n.191, pred[]{:T(512)S(6)} %eq.79, bf16[1,4,64,2048]{3,2,1,0:T(8,128)(2,1)} %param.24), kind=kLoop, calls=%fused_computation.50 | loop fusion | flops 262144 | bytes 1048581 | tf_op jit(solution)/shard_map/jit(_where)/select_n | solution.py:14
  18.3 0.0 all-reduce.3.cloned.1.call-update
  18.4 0.1 select_reduce_fusion.1
  18.5 0.1 broadcast_compare_fusion.1
  18.6 0.3 multiply_cosine_fusion
  18.9 75.1 %all-reduce.3.cloned.1.call-done = (bf16[2,64,256]{2,1,0:T(8,128)(2,1)}, bf16[192,2048]{1,0:T(8,128)(2,1)}, bf16[64,2048]{1,0:T(8,128)(2,1)}, bf16[64,2048]{1,0:T(8,128)(2,1)}, bf16[64,2048]{1,0:T(8,128)(2,1)}) async-done(((bf16[2,64,256]{2,1,0:T(8,128)(2,1)}, bf16[192,2048]{1,0:T(8,128)(2,1)}, bf16[64,2048]{1,0:T(8,128)(2,1)}, bf16[64,2048]{1,0:T(8,128)(2,1)}, bf16[64,2048]{1,0:T(8,128)(2,1)}), ...) | async-done | bytes 1638416 | tf_op jit(solution)/shard_map/psum | solution.py:15
  94.0 1.5 convolution_bitcast_fusion
  95.5 12.3 %psum.50 = bf16[128,192]{0,1:T(8,128)(2,1)S(1)} all-reduce(f32[128,192]{0,1:T(8,128)S(1)} %convolution_bitcast_fusion), channel_id=1, replica_groups=mesh['groups'=2,'ctx'=4,'tp'=4] {'tp'}, use_global_device_ids=true, to_apply=%region_1.2 | all-reduce | flops 24576 | bytes 147456 | tf_op jit(solution)/shard_map/psum | solution.py:103
  107.9 1.0 fusion.15
  108.9 1.3 fusion.12
  110.2 0.2 copy.43
  110.4 0.5 subtract_convert_fusion
  110.9 0.1 copy.26
  111.1 0.1 copy.27
  111.2 0.0 copy-done.7
  111.2 0.2 convolution_add_fusion.4
  111.4 0.1 reshape.263
  111.5 0.2 fusion.34
  111.7 0.3 pad_maximum_fusion
  112.1 0.1 pad_maximum_fusion.1
  112.2 0.3 fusion.35
  112.5 0.2 fusion.17
  112.7 0.5 convolution_add_fusion.2
  113.3 22.6 %while.24 = (s32[]{:T(128)}, bf16[128,2,128]{2,0,1:T(8,128)(2,1)S(1)}, bf16[128,2,128]{2,0,1:T(8,128)(2,1)S(1)}, f32[2,8,128]{2,1,0:T(8,128)S(1)}, f32[2,8,128]{...) while((s32[]{:T(128)}, ...), condition=%wide.region_11.12_spmd, body=%wide.region_7.11_spmd.sunk | while | flops 137128592 | bytes 6885278 | solution.py:155
  113.3 0.2 collective-permute-start
  113.5 1.8 %collective-permute-start.1 = (bf16[128,2,128]{2,0,1:T(8,128)(2,1)S(1)}, bf16[128,2,128]{2,0,1:T(8,128)(2,1)S(1)}, u32[]{:S(2)}, u32[]{:S(2)}) collective-permute-start(bf16[128,2,128]{2,0,1:T(8,128)(2,1)S(1)} %get-tuple-element.440), channel_id=1, source_target_pairs={{0,4},{4,8},{8,12},{12,0},{1,5},{5,9},{9,13},{13,1},{2,6},{6,10},{... | collective-permute-start | bytes 196616 | tf_op jit(solution)/shard_map/while/body/eval_jaxpr/ppermute | solution.py:21
  115.3 0.1 select_reduce_fusion.3
  115.4 0.1 broadcast_compare_fusion.3
  115.5 3.9 %collective-permute-done = bf16[128,2,128]{2,0,1:T(8,128)(2,1)S(1)} collective-permute-done((bf16[128,2,128]{2,0,1:T(8,128)(2,1)S(1)}, bf16[128,2,128]{2,0,1:T(8,128)(2,1)S(1)}, u32[]{:S(2)}, u32[]{:S(2)}) %collective-permute-start) | collective-permute-done | bytes 65568 | tf_op jit(solution)/shard_map/while/body/eval_jaxpr/ppermute | solution.py:21
  119.4 0.3 fusion.56
  119.7 0.2 fusion.57
  120.0 0.1 collective-permute-done.1
  120.1 0.7 convolution_add_fusion.6
  120.8 0.1 collective-permute-start
  120.9 0.1 collective-permute-start.1
  121.0 0.1 select_reduce_fusion.3
  121.1 0.1 broadcast_compare_fusion.3
  121.2 5.7 %collective-permute-done = bf16[128,2,128]{2,0,1:T(8,128)(2,1)S(1)} collective-permute-done((bf16[128,2,128]{2,0,1:T(8,128)(2,1)S(1)}, bf16[128,2,128]{2,0,1:T(8,128)(2,1)S(1)}, u32[]{:S(2)}, u32[]{:S(2)}) %collective-permute-start) | collective-permute-done | bytes 65568 | tf_op jit(solution)/shard_map/while/body/eval_jaxpr/ppermute | solution.py:21
  126.9 0.3 fusion.56
  127.3 0.2 fusion.57
  127.5 0.1 collective-permute-done.1
  127.6 0.7 convolution_add_fusion.6
  128.3 0.1 collective-permute-start
  128.4 0.3 collective-permute-start.1
  128.7 0.1 select_reduce_fusion.3
  128.8 0.1 broadcast_compare_fusion.3
  128.9 5.5 %collective-permute-done = bf16[128,2,128]{2,0,1:T(8,128)(2,1)S(1)} collective-permute-done((bf16[128,2,128]{2,0,1:T(8,128)(2,1)S(1)}, bf16[128,2,128]{2,0,1:T(8,128)(2,1)S(1)}, u32[]{:S(2)}, u32[]{:S(2)}) %collective-permute-start) | collective-permute-done | bytes 65568 | tf_op jit(solution)/shard_map/while/body/eval_jaxpr/ppermute | solution.py:21
  134.4 0.3 fusion.56
  134.8 0.2 fusion.57
  135.0 0.1 collective-permute-done.1
  135.2 0.7 convolution_add_fusion.6
  135.9 0.3 fusion.21
  136.2 0.3 copy.31
  136.6 0.1 copy.53
  136.7 0.1 copy-done.4
  136.8 0.3 convolution_convert_fusion.1
  137.1 10.3 %psum.54 = bf16[128,64]{1,0:T(8,128)(2,1)S(1)} all-reduce(bf16[128,64]{1,0:T(8,128)(2,1)S(1)} %convolution_convert_fusion.1), channel_id=1, replica_groups=mesh['groups'=2,'ctx'=4,'tp'=4] {'tp'}, use_global_device_ids=true, to_apply=%region_13.14 | all-reduce | flops 8192 | bytes 32768 | tf_op jit(solution)/shard_map/psum | solution.py:167
  147.4 1.1 convolution_convert_fusion
  (44 shorter events, 0.3 us)
Async XLA Ops:
  7.2 86.9 %copy-start = (bf16[128,2048]{1,0:T(8,128)(2,1)S(1)}, bf16[128,2048]{1,0:T(8,128)(2,1)}, u32[]{:S(2)}) copy-start(bf16[128,2048]{1,0:T(8,128)(2,1)} %param.14) | copy-start | bytes 1572868
  7.2 11.2 %copy-start.8 = (s32[8]{0:T(128)S(1)}, s32[8]{0:T(128)}, u32[]{:S(2)}) copy-start(s32[8]{0:T(128)} %param.18) | copy-start | bytes 100
  7.2 86.8 %all-reduce.3.cloned.1.call-start = ((), (), s32[]{:S(2)}) async-start(), calls=%async_computation | async-start | bytes 3276800 | tf_op jit(solution)/shard_map/psum | solution.py:15
  11.1 96.8 %copy-start.6 = (bf16[128,256]{1,0:T(8,128)(2,1)S(1)}, bf16[128,256]{1,0:T(8,128)(2,1)}, u32[]{:S(2)}) copy-start(bf16[128,256]{1,0:T(8,128)(2,1)} %param.17) | copy-start | bytes 196612
  13.3 95.6 %copy-start.2 = (bf16[128,2048]{1,0:T(8,128)(2,1)S(1)}, bf16[128,2048]{1,0:T(8,128)(2,1)}, u32[]{:S(2)}) copy-start(bf16[128,2048]{1,0:T(8,128)(2,1)} %param.15) | copy-start | bytes 1572868
  110.4 0.9 copy-start.5
  110.4 0.9 copy-start.7
  113.3 6.1 %collective-permute-start = (bf16[128,2,128]{2,0,1:T(8,128)(2,1)S(1)}, bf16[128,2,128]{2,0,1:T(8,128)(2,1)S(1)}, u32[]{:S(2)}, u32[]{:S(2)}) collective-permute-start(bf16[128,2,128]{2,0,1:T(8,128)(2,1)S(1)} %get-tuple-element.439), channel_id=1, source_target_pairs={{0,4},{4,8},{8,12},{12,0},{1,5},{5,9},{9,13},{13,1},{2,6},{6,10},{... | collective-permute-start | bytes 196616 | tf_op jit(solution)/shard_map/while/body/eval_jaxpr/ppermute | solution.py:21
  113.5 6.6 %collective-permute-start.1 = (bf16[128,2,128]{2,0,1:T(8,128)(2,1)S(1)}, bf16[128,2,128]{2,0,1:T(8,128)(2,1)S(1)}, u32[]{:S(2)}, u32[]{:S(2)}) collective-permute-start(bf16[128,2,128]{2,0,1:T(8,128)(2,1)S(1)} %get-tuple-element.440), channel_id=1, source_target_pairs={{0,4},{4,8},{8,12},{12,0},{1,5},{5,9},{9,13},{13,1},{2,6},{6,10},{... | collective-permute-start | bytes 196616 | tf_op jit(solution)/shard_map/while/body/eval_jaxpr/ppermute | solution.py:21
  120.8 6.1 %collective-permute-start = (bf16[128,2,128]{2,0,1:T(8,128)(2,1)S(1)}, bf16[128,2,128]{2,0,1:T(8,128)(2,1)S(1)}, u32[]{:S(2)}, u32[]{:S(2)}) collective-permute-start(bf16[128,2,128]{2,0,1:T(8,128)(2,1)S(1)} %get-tuple-element.439), channel_id=1, source_target_pairs={{0,4},{4,8},{8,12},{12,0},{1,5},{5,9},{9,13},{13,1},{2,6},{6,10},{... | collective-permute-start | bytes 196616 | tf_op jit(solution)/shard_map/while/body/eval_jaxpr/ppermute | solution.py:21
  120.9 6.8 %collective-permute-start.1 = (bf16[128,2,128]{2,0,1:T(8,128)(2,1)S(1)}, bf16[128,2,128]{2,0,1:T(8,128)(2,1)S(1)}, u32[]{:S(2)}, u32[]{:S(2)}) collective-permute-start(bf16[128,2,128]{2,0,1:T(8,128)(2,1)S(1)} %get-tuple-element.440), channel_id=1, source_target_pairs={{0,4},{4,8},{8,12},{12,0},{1,5},{5,9},{9,13},{13,1},{2,6},{6,10},{... | collective-permute-start | bytes 196616 | tf_op jit(solution)/shard_map/while/body/eval_jaxpr/ppermute | solution.py:21
  128.3 6.1 %collective-permute-start = (bf16[128,2,128]{2,0,1:T(8,128)(2,1)S(1)}, bf16[128,2,128]{2,0,1:T(8,128)(2,1)S(1)}, u32[]{:S(2)}, u32[]{:S(2)}) collective-permute-start(bf16[128,2,128]{2,0,1:T(8,128)(2,1)S(1)} %get-tuple-element.439), channel_id=1, source_target_pairs={{0,4},{4,8},{8,12},{12,0},{1,5},{5,9},{9,13},{13,1},{2,6},{6,10},{... | collective-permute-start | bytes 196616 | tf_op jit(solution)/shard_map/while/body/eval_jaxpr/ppermute | solution.py:21
  128.4 6.8 %collective-permute-start.1 = (bf16[128,2,128]{2,0,1:T(8,128)(2,1)S(1)}, bf16[128,2,128]{2,0,1:T(8,128)(2,1)S(1)}, u32[]{:S(2)}, u32[]{:S(2)}) collective-permute-start(bf16[128,2,128]{2,0,1:T(8,128)(2,1)S(1)} %get-tuple-element.440), channel_id=1, source_target_pairs={{0,4},{4,8},{8,12},{12,0},{1,5},{5,9},{9,13},{13,1},{2,6},{6,10},{... | collective-permute-start | bytes 196616 | tf_op jit(solution)/shard_map/while/body/eval_jaxpr/ppermute | solution.py:21
  135.9 1.0 copy-start.4
  135.9 11.5 %copy-start.3 = (bf16[64,2048]{1,0:T(8,128)(2,1)S(1)}, bf16[64,2048]{1,0:T(8,128)(2,1)}, u32[]{:S(2)}) copy-start(bf16[64,2048]{1,0:T(8,128)(2,1)} %get-tuple-element.332) | copy-start | bytes 786436
  136.7 11.7 %copy-start.1 = (bf16[16,8,16,128]{3,1,2,0:T(8,128)(2,1)}, bf16[16,8,16,128]{3,1,2,0:T(8,128)(2,1)S(1)}, u32[]{:S(2)}) copy-start(bf16[16,8,16,128]{3,1,2,0:T(8,128)(2,1)S(1)} %copy.53) | copy-start | bytes 1572868
Sparse Core Ops, SparseCore 0:
  18.5 75.4 all-reduce.2
where the time goes:
time: 156 us; the launch traced here: 155 us
  waiting for transfers between devices  90.7 us (58%)
  blocking collectives  22.6 us (14%)
  between operations  17 us (11%)
  other arithmetic  10.5 us (7%)
  matrix products  9.09 us (6%)
  local copies, waits for them, and re-layouts  2.65 us (2%)
  starting transfers between devices  2.6 us (2%)
    psum x1, waiting for transfers between devices, spread(): return lax.psum(kept, axis)  75.1 us
    ppermute x6, waiting for transfers between devices, from_behind(): return lax.ppermute(value, axis, pairs)  15.5 us
    psum x1, blocking collectives, shards(): rank_projection = lax.psum(partial_value, 'tp').astype(jnp.bfloat16)  12.3 us
    psum x1, blocking collectives, shards(): out_low = lax.psum(out_partial.astype(jnp.bfloat16), 'tp')  10.3 us
    select_n x4, other arithmetic, spread(): jnp.where(lax.axis_index(axis) == source, value, 0).astype(value.dtype)  7.19 us
  transfers between devices with their start and end apart: 7, of which 7 were waited for; matrix products, arithmetic and copies ran while one was open for 2% of the time, Pallas kernels for 0%

commit v1 on v0

v1 whole, which is shorter than its diff:
```python
import functools

import jax
import jax.numpy as jnp
import numpy as np
from jax import lax
from jax.experimental import pallas as pl
from jax.experimental.pallas import tpu as pltpu
from jax.sharding import PartitionSpec as P

HEAD_SIZE = 128
ADAPTER_RANK = 64
NEG_BIG = -1e30
NT = (((1,), (1,)), ((), ()))
PARTS = 8


def kernel(
    n,
    tp,
    group_size,
    order_ref,
    version_ref,
    publisher_ref,
    frequency_ref,
    hidden_hbm,
    base_q_hbm,
    base_k_hbm,
    base_v_hbm,
    down_hbm,
    up_q_hbm,
    up_kv_hbm,
    outer_down_hbm,
    outer_up_hbm,
    attended_ref,
    adapted_ref,
    hidden,
    base_q,
    base_k,
    base_v,
    own,
    in_r,
    in_l,
    out_r,
    out_l,
    final,
    queries,
    kv_all,
    bias,
    cosine,
    sine,
    partial,
    rs_buf,
    rank_low,
    partial2,
    rs_buf2,
    out_low,
    own_sem,
    base_sem,
    send_r,
    recv_r,
    send_l,
    recv_l,
    kv_send,
    kv_recv,
    rs_send,
    rs_recv,
    ag_send,
    ag_recv,
    rs2_send,
    rs2_recv,
    ag2_send,
    ag2_recv,
):
    me = lax.axis_index("ctx")
    lane = lax.axis_index("tp")
    count, _, rank, cw = own.shape
    rows, width = hidden.shape
    parts = width // cw
    n_down = down_hbm.shape[2] // rank
    first_k = n_down * parts
    first_q = first_k + 2
    first_od = first_q + parts
    first_ou = first_od + parts
    heads_per_chunk = cw // HEAD_SIZE
    groups = kv_all.shape[1] // 2
    share = rows // tp

    def own_copy(src, c):
        return pltpu.make_async_copy(src, own.at[c], own_sem.at[c])

    def cols(k):
        return pl.ds(pl.multiple_of(k * cw, cw), cw)

    def load_down(k, _):
        for r in range(n_down):
            own_copy(
                down_hbm.at[0, :, pl.ds(r * rank, rank), cols(k)], k * n_down + r
            ).start()
        return 0

    base_copies = [
        pltpu.make_async_copy(src, dst, base_sem.at[i])
        for i, (src, dst) in enumerate(
            [(hidden_hbm, hidden), (base_q_hbm, base_q), (base_k_hbm, base_k), (base_v_hbm, base_v)]
        )
    ]

    barrier = pltpu.get_barrier_semaphore()

    def greet(axis, own_index, size):
        def one(d, _):
            pl.semaphore_signal(
                barrier,
                inc=1,
                device_id={axis: lax.rem(own_index + d, size)},
                device_id_type=pl.DeviceIdType.MESH,
            )
            return 0

        lax.fori_loop(1, size, one, 0)

    greet("ctx", me, n)
    greet("tp", lane, tp)

    load_down(0, 0)
    base_copies[0].start()
    lax.fori_loop(1, parts, load_down, 0)
    for c in range(2):
        own_copy(up_kv_hbm.at[0, :, c], first_k + c).start()

    def load_wide(k, _):
        own_copy(up_q_hbm.at[0, :, :, cols(k)], first_q + k).start()
        own_copy(outer_down_hbm.at[0, :, :, cols(k)], first_od + k).start()
        own_copy(outer_up_hbm.at[0, :, :, cols(k)], first_ou + k).start()
        return 0

    lax.fori_loop(0, parts, load_wide, 0)
    for copy in base_copies[1:]:
        copy.start()

    source = publisher_ref[0]
    chosen = version_ref[source]
    is_source = source == me
    from_left = source <= me

    pl.semaphore_wait(barrier, n - 1 + tp - 1)

    def hop_right(c):
        return pltpu.make_async_remote_copy(
            src_ref=out_r.at[c],
            dst_ref=in_r.at[c],
            send_sem=send_r.at[c],
            recv_sem=recv_r.at[c],
            device_id={"ctx": lax.rem(me + 1, n)},
            device_id_type=pl.DeviceIdType.MESH,
        )

    def hop_left(c):
        return pltpu.make_async_remote_copy(
            src_ref=out_l.at[c],
            dst_ref=in_l.at[c],
            send_sem=send_l.at[c],
            recv_sem=recv_l.at[c],
            device_id={"ctx": lax.rem(me + n - 1, n)},
            device_id_type=pl.DeviceIdType.MESH,
        )

    def stored_chunk(c):
        value = own[c, 0]
        for e in range(1, own.shape[1]):
            value = jnp.where(chosen == e, own[c, e], value)
        return value

    def relay(t):
        @pl.when(t < count)
        def _():
            own_copy(own.at[t], t).wait()

        right = t - me

        @pl.when((right >= 0) & (right < count))
        def _():
            @pl.when(me == 0)
            def _():
                out_r[right] = stored_chunk(right)

            @pl.when(me > 0)
            def _():
                hop_right(right).wait_recv()
                out_r[right] = jnp.where(is_source, stored_chunk(right), in_r[right])

            @pl.when(me < n - 1)
            def _():
                hop_right(right).start()

        left = t - (n - 1 - me)

        @pl.when((left >= 0) & (left < count))
        def _():
            @pl.when(me == n - 1)
            def _():
                out_l[left] = stored_chunk(left)

            @pl.when(me < n - 1)
            def _():
                hop_left(left).wait_recv()
                out_l[left] = jnp.where(is_source, stored_chunk(left), in_l[left])

            @pl.when(me > 0)
            def _():
                hop_left(left).start()

        done = t - (n - 1)

        @pl.when(done >= 0)
        def _():
            final[done] = jnp.where(from_left, out_r[done], out_l[done])

    def relay_range(start, stop):
        def one(t, _):
            relay(t)
            return 0

        lax.fori_loop(start, stop, one, 0)

    def tp_copy(src, dst, send, recv, d, sem):
        return pltpu.make_async_remote_copy(
            src_ref=src,
            dst_ref=dst,
            send_sem=send.at[d],
            recv_sem=recv.at[sem],
            device_id={"tp": lax.rem(lane + d, tp)},
            device_id_type=pl.DeviceIdType.MESH,
        )

    def row_share(j):
        return pl.ds(pl.multiple_of(j * share, share), share)

    def each_peer(fn):
        def one(d, _):
            fn(d, lax.rem(lane + d, tp))
            return 0

        lax.fori_loop(1, tp, one, 0)

    def scatter_start(src, buf, send, recv):
        each_peer(
            lambda d, j: tp_copy(
                src.at[row_share(j)], buf.at[lane], send, recv, d, lane
            ).start()
        )
        buf[lane] = src[row_share(lane)]

    def scatter_wait(src, buf, send, recv):
        each_peer(
            lambda d, j: tp_copy(
                src.at[row_share(j)], buf.at[j], send, recv, d, j
            ).wait()
        )
        return jnp.sum(buf[...], axis=0)

    def gather_start(value, buf, send, recv):
        mine = buf.at[row_share(lane)]
        mine[...] = value.astype(buf.dtype)
        each_peer(lambda d, j: tp_copy(mine, mine, send, recv, d, lane).start())

    def gather_wait(buf, send, recv):
        each_peer(
            lambda d, j: tp_copy(
                buf.at[row_share(lane)], buf.at[row_share(j)], send, recv, d, j
            ).wait()
        )

    relay_range(0, n - 1)
    blocks = order_ref.shape[0]
    block_rows = rows * n // blocks
    per_device = blocks // n
    token = lax.broadcasted_iota(jnp.int32, (rows, HEAD_SIZE), 0)
    stored = jnp.zeros((rows, HEAD_SIZE), jnp.int32)
    for b in range(per_device):
        stored = jnp.where(
            token // block_rows == b, order_ref[me * per_device + b], stored
        )
    position = stored * block_rows + token % block_rows
    angle = position.astype(jnp.float32) * frequency_ref[...]
    half = lax.broadcasted_iota(jnp.int32, (rows, HEAD_SIZE), 1) < HEAD_SIZE // 2
    cosine[...] = jnp.cos(angle)
    sine_all = jnp.sin(angle)
    sine[...] = jnp.where(half, -sine_all, sine_all)
    key = lax.broadcasted_iota(jnp.int32, (rows, block_rows * 2), 1)
    query_position = jnp.concatenate(
        [position] * (block_rows * 2 // HEAD_SIZE), axis=1
    )
    for b in range(0, blocks, 2):
        key_position = (
            jnp.where(key < block_rows, order_ref[b], order_ref[b + 1]) * block_rows
            + key % block_rows
        )
        bias[:, b * block_rows : (b + 2) * block_rows] = jnp.where(
            key_position <= query_position, 0.0, NEG_BIG
        )
    partial[...] = jnp.zeros_like(partial)
    partial2[...] = jnp.zeros_like(partial2)
    base_copies[0].wait()

    def down_step(k, _):
        for r in range(n_down):
            relay(n - 1 + k * n_down + r)
        weight = final[pl.ds(k * n_down, n_down)].reshape(n_down * rank, cw)
        partial[:, : n_down * rank] += lax.dot_general(
            hidden[:, cols(k)], weight, NT, preferred_element_type=jnp.float32
        )
        return 0

    lax.fori_loop(0, parts, down_step, 0)
    t = n - 1 + first_k
    scatter_start(partial, rs_buf, rs_send, rs_recv)
    relay_range(t, t + 2)
    gather_start(
        scatter_wait(partial, rs_buf, rs_send, rs_recv), rank_low, ag_send, ag_recv
    )
    relay_range(t + 2, t + 4)
    for copy in base_copies[1:]:
        copy.wait()
    gather_wait(rank_low, ag_send, ag_recv)

    def rotate(values):
        return values * cosine[...] + pltpu.roll(values, HEAD_SIZE // 2, 1) * sine[...]

    low = rank_low[...]
    keys = base_k[...].astype(jnp.float32) + jnp.dot(
        low[:, rank : 2 * rank], final[first_k], preferred_element_type=jnp.float32
    )
    values = base_v[...].astype(jnp.float32) + jnp.dot(
        low[:, 2 * rank : 3 * rank],
        final[first_k + 1],
        preferred_element_type=jnp.float32,
    )
    for g in range(groups):
        span = slice(g * HEAD_SIZE, (g + 1) * HEAD_SIZE)
        kv_all[me, g] = rotate(keys[:, span]).astype(jnp.bfloat16)
        kv_all[me, groups + g] = values[:, span].astype(jnp.bfloat16)

    def kv_copy(d, place):
        return pltpu.make_async_remote_copy(
            src_ref=kv_all.at[me],
            dst_ref=kv_all.at[place],
            send_sem=kv_send.at[d],
            recv_sem=kv_recv.at[place],
            device_id={"ctx": lax.rem(me + d, n)},
            device_id_type=pl.DeviceIdType.MESH,
        )

    def kv_start(d, _):
        kv_copy(d, me).start()
        return 0

    def kv_wait(d, _):
        kv_copy(d, lax.rem(me + d, n)).wait()
        return 0

    lax.fori_loop(1, n, kv_start, 0)

    low_q = low[:, :rank]

    def query_step(j, _):
        relay(t + 4 + j)
        adapted_q = base_q[:, cols(j)].astype(jnp.float32) + jnp.dot(
            low_q, final[first_q + j], preferred_element_type=jnp.float32
        )
        for h in range(heads_per_chunk):
            span = slice(h * HEAD_SIZE, (h + 1) * HEAD_SIZE)
            queries[j, :, span] = rotate(adapted_q[:, span]).astype(jnp.bfloat16)
        return 0

    lax.fori_loop(0, parts, query_step, 0)
    relay_range(t + 4 + parts, n - 1 + first_ou)
    lax.fori_loop(1, n, kv_wait, 0)

    def head_step(j, _):
        relay(n - 1 + first_ou + j)
        for h in range(heads_per_chunk):
            span = slice(h * HEAD_SIZE, (h + 1) * HEAD_SIZE)
            group = (j * heads_per_chunk + h) // group_size
            key_block = kv_all[:, group].reshape(n * rows, HEAD_SIZE)
            value_block = kv_all[:, groups + group].reshape(n * rows, HEAD_SIZE)
            scores = (
                lax.dot_general(
                    queries[j, :, span], key_block, NT, preferred_element_type=jnp.float32
                )
                * HEAD_SIZE ** (-0.5)
                + bias[...]
            )
            raw = jnp.exp(scores - jnp.max(scores, axis=1, keepdims=True))
            totals = jnp.sum(raw, axis=1, keepdims=True)
            mixed = jnp.dot(
                raw.astype(jnp.bfloat16), value_block, preferred_element_type=jnp.float32
            )
            place = pl.ds(pl.multiple_of(j * cw + h * HEAD_SIZE, HEAD_SIZE), HEAD_SIZE)
            attended_ref[:, place] = (mixed / totals).astype(jnp.bfloat16)
        partial2[:, :rank] += lax.dot_general(
            attended_ref[:, cols(j)],
            final[first_od + j],
            NT,
            preferred_element_type=jnp.float32,
        )
        return 0

    lax.fori_loop(0, parts, head_step, 0)
    scatter_start(partial2, rs_buf2, rs2_send, rs2_recv)
    gather_start(
        scatter_wait(partial2, rs_buf2, rs2_send, rs2_recv), out_low, ag2_send, ag2_recv
    )

    def drain(c, _):
        @pl.when(me < n - 1)
        def _():
            hop_right(c).wait_send()

        @pl.when(me > 0)
        def _():
            hop_left(c).wait_send()

        return 0

    lax.fori_loop(0, count, drain, 0)
    gather_wait(out_low, ag2_send, ag2_recv)
    outer = out_low[:, :rank]

    def up_step(j, _):
        adapted_ref[:, cols(j)] = jnp.dot(
            outer, final[first_ou + j], preferred_element_type=jnp.float32
        ).astype(jnp.bfloat16)
        return 0

    lax.fori_loop(0, parts, up_step, 0)


def shards(
    n,
    tp,
    hidden,
    base_query_rows,
    base_key_rows,
    base_value_rows,
    stored_block_order,
    version,
    publisher,
    adapter_down_weight,
    adapter_up_query,
    adapter_up_key_value,
    output_down_weight,
    output_up_weight,
):
    rows, width = hidden.shape
    versions, rank = adapter_up_query.shape[1:3]
    kv_width = base_key_rows.shape[1]
    groups = kv_width // HEAD_SIZE
    cw = width // PARTS
    count = adapter_down_weight.shape[2] // rank * PARTS + 2 + 3 * PARTS
    half = np.arange(HEAD_SIZE // 2, dtype=np.float32) * np.float32(2.0) / np.float32(HEAD_SIZE)
    frequency = np.power(np.float32(500000.0), -half).astype(np.float32)
    frequency = jnp.asarray(np.concatenate([frequency, frequency])[None, :])
    bf16, f32 = jnp.bfloat16, jnp.float32
    chunk = pltpu.VMEM((count, rank, cw), bf16)
    dma = pltpu.SemaphoreType.DMA
    share = rows // tp
    smem = pl.BlockSpec(memory_space=pltpu.SMEM)
    vmem = pl.BlockSpec(memory_space=pltpu.VMEM)
    hbm = pl.BlockSpec(memory_space=pl.ANY)
    out = jax.ShapeDtypeStruct((rows, width), bf16)
    return pl.pallas_call(
        functools.partial(kernel, n, tp, width // kv_width),
        out_shape=(out, out),
        in_specs=[smem] * 3 + [vmem] + [hbm] * 9,
        out_specs=(vmem, vmem),
        scratch_shapes=[
            pltpu.VMEM((rows, width), bf16),
            pltpu.VMEM((rows, width), bf16),
            pltpu.VMEM((rows, kv_width), bf16),
            pltpu.VMEM((rows, kv_width), bf16),
            pltpu.VMEM((count, versions, rank, cw), bf16),
            chunk,
            chunk,
            chunk,
            chunk,
            chunk,
            pltpu.VMEM((PARTS, rows, cw), bf16),
            pltpu.VMEM((n, 2 * groups, rows, HEAD_SIZE), bf16),
            pltpu.VMEM((rows, n * rows), f32),
            pltpu.VMEM((rows, HEAD_SIZE), f32),
            pltpu.VMEM((rows, HEAD_SIZE), f32),
            pltpu.VMEM((rows, 2 * HEAD_SIZE), f32),
            pltpu.VMEM((tp, share, 2 * HEAD_SIZE), f32),
            pltpu.VMEM((rows, 2 * HEAD_SIZE), bf16),
            pltpu.VMEM((rows, HEAD_SIZE), f32),
            pltpu.VMEM((tp, share, HEAD_SIZE), f32),
            pltpu.VMEM((rows, HEAD_SIZE), bf16),
            dma((count,)),
            dma((4,)),
            dma((count,)),
            dma((count,)),
            dma((count,)),
            dma((count,)),
            dma((n,)),
            dma((n,)),
        ]
        + [dma((tp,))] * 8,
        compiler_params=pltpu.CompilerParams(
            collective_id=0, has_side_effects=True, vmem_limit_bytes=48 * 1024 * 1024
        ),
    )(
        stored_block_order,
        version,
        publisher,
        frequency,
        hidden,
        base_query_rows,
        base_key_rows,
        base_value_rows,
        adapter_down_weight,
        adapter_up_query,
        adapter_up_key_value,
        output_down_weight,
        output_up_weight,
    )


def solution(mesh):
    placed = (
        P(("groups", "ctx"), "tp"),
        P(("groups", "ctx"), "tp"),
        P(("groups", "ctx"), "tp"),
        P(("groups", "ctx"), "tp"),
        P("groups"),
        P("groups"),
        P("groups"),
        P("ctx", None, None, "tp"),
        P("ctx", None, None, "tp"),
        P("ctx", None, None, None, "tp"),
        P("ctx", None, None, "tp"),
        P("ctx", None, None, "tp"),
    )
    return jax.shard_map(
        functools.partial(shards, mesh.shape["ctx"], mesh.shape["tp"]),
        mesh=mesh,
        in_specs=placed,
        out_specs=(P(("groups", "ctx"), "tp"), P(("groups", "ctx"), "tp")),
        check_vma=False,
    )
```

time: 156 us -> 171 us (1.096)
  Pallas kernels: 0 us -> 158 us
  waiting for transfers between devices: 90.7 us -> 0 us
  blocking collectives: 22.6 us -> 0 us
  between operations: 17 us -> 1.31 us
  other arithmetic: 10.5 us -> 0 us
  local copies, waits for them, and re-layouts: 2.65 us -> 11.9 us
  matrix products: 9.09 us -> 0 us
  starting transfers between devices: 2.6 us -> 0 us
    pallas_call x0 -> x1, Pallas kernels: none -> 158 us  [shards(): pl.pallas_call(functools.partial(kernel, n, tp, width // kv_width), out_s...]
    psum x1 -> x0, waiting for transfers between devices: 75.1 us -> none  [spread(): return lax.psum(kept, axis)]
    psum x2 -> x0, blocking collectives: 22.6 us -> none  [the longest x1 12.3 us: shards(): rank_projection = lax.psum(partial_value, 'tp').astype(jnp.bfloat16)]
    ppermute x6 -> x0, waiting for transfers between devices: 15.5 us -> none  [from_behind(): return lax.ppermute(value, axis, pairs)]
    unnamed x20 -> x24, local copies, waits for them, and re-layouts: 0.45 us -> 11.9 us
    dot_general x14 -> x0, matrix products: 9.09 us -> none  [the longest x4 2.58 us: attend_block(): jnp.einsum('kgts,skd->kgtd', raw_scores.astype(jnp.bfloat16), adapted_val...]
    select_n x8 -> x0, other arithmetic: 7.23 us -> none  [the longest x4 7.19 us: spread(): jnp.where(lax.axis_index(axis) == source, value, 0).astype(value.dtype)]
    ppermute x6 -> x0, starting transfers between devices: 2.57 us -> none  [from_behind(): return lax.ppermute(value, axis, pairs)]
  transfers between devices with their start and end apart: 7 -> 0, of which waited for: 7 -> 0; matrix products, arithmetic and copies ran while one was open for 2% -> 0% of each run, Pallas kernels for 0% -> 0%
where the time goes in v1:
time: 171 us
  Pallas kernels  158 us (92%)
  local copies, waits for them, and re-layouts  11.9 us (7%)
    pallas_call x1, Pallas kernels, shards(): pl.pallas_call(functools.partial(kernel, n, tp, width // kv_width), out_s...  158 us
    unnamed x24, local copies, waits for them, and re-layouts  11.9 us

profile of v1, /device:TPU:0, one launch (start us, length us, event | category | flops | bytes accessed | tf_op | source)
XLA Modules:
  0.0 171.0 jit_solution(10512773367579586140)
XLA Ops:
  1.3 0.0 copy-start
  1.3 1.2 copy-done
  2.5 0.0 copy-start.1
  2.5 1.2 copy-done.1
  3.7 0.0 copy-start.2
  3.7 1.2 copy-done.2
  5.0 0.0 copy-start.3
  5.0 1.0 copy-done.3
  6.0 0.0 copy-start.4
  6.0 1.0 copy-done.4
  7.0 0.0 copy-start.5
  7.0 0.9 copy-done.5
  8.0 0.0 copy-start.6
  8.0 0.8 copy-done.6
  8.8 0.0 copy-start.7
  8.8 0.8 copy-done.7
  9.7 0.0 copy-start.8
  9.7 0.7 copy-done.8
  10.3 0.0 copy-start.9
  10.3 0.7 copy-done.9
  11.0 0.0 copy-start.10
  11.0 0.7 copy-done.10
  11.6 157.8 %shard_map.140 = (bf16[128,2048]{1,0:T(8,128)(2,1)S(1)}, bf16[128,2048]{1,0:T(8,128)(2,1)S(1)}) custom-call(s32[8]{0:T(128)S(1)} %copy-done.8, s32[4]{0:T(128)S(1)} %copy-done.9, s32[1]{0:T(128)S(6)} %copy.17.publisher_ref, f32[1,128]{1,0:T(1,128)S(1)} %copy-done.10, bf16[128,2048]{1,0:T(8,128)(2,1)S(1)} %copy-done.3, bf16[128,2048]{1,0:T(8,128)(2,1)S(1)} %copy-done.4, ...), custom_call_target="tpu_custom_call" | custom-call | tf_op jit(solution)/shard_map/pallas_call | solution.py:473
  169.4 0.8 copy.18
  170.2 0.8 copy.19
Async XLA Ops:
  1.3 1.2 copy-start
  2.5 1.2 copy-start.1
  3.7 1.2 copy-start.2
  5.0 1.0 copy-start.3
  6.0 1.0 copy-start.4
  7.0 0.9 copy-start.5
  8.0 0.8 copy-start.6
  8.8 0.8 copy-start.7
  9.7 0.7 copy-start.8
  10.3 0.7 copy-start.9
  11.0 0.7 copy-start.10

commit v2 on v1

--- a/solution.py
+++ b/solution.py
@@ -13,6 +13,7 @@
 NEG_BIG = -1e30
 NT = (((1,), (1,)), ((), ()))
 PARTS = 8
+LAG = 4
 
 
 def kernel(
@@ -85,6 +86,7 @@
     heads_per_chunk = cw // HEAD_SIZE
     groups = kv_all.shape[1] // 2
     share = rows // tp
+    fill = (n - 1) * LAG
 
     def own_copy(src, c):
         return pltpu.make_async_copy(src, own.at[c], own_sem.at[c])
@@ -177,7 +179,7 @@
         def _():
             own_copy(own.at[t], t).wait()
 
-        right = t - me
+        right = t - me * LAG
 
         @pl.when((right >= 0) & (right < count))
         def _():
@@ -194,7 +196,7 @@
             def _():
                 hop_right(right).start()
 
-        left = t - (n - 1 - me)
+        left = t - (n - 1 - me) * LAG
 
         @pl.when((left >= 0) & (left < count))
         def _():
@@ -211,7 +213,7 @@
             def _():
                 hop_left(left).start()
 
-        done = t - (n - 1)
+        done = t - fill
 
         @pl.when(done >= 0)
         def _():
@@ -272,7 +274,7 @@
             ).wait()
         )
 
-    relay_range(0, n - 1)
+    relay_range(0, fill)
     blocks = order_ref.shape[0]
     block_rows = rows * n // blocks
     per_device = blocks // n
@@ -306,7 +308,7 @@
 
     def down_step(k, _):
         for r in range(n_down):
-            relay(n - 1 + k * n_down + r)
+            relay(fill + k * n_down + r)
         weight = final[pl.ds(k * n_down, n_down)].reshape(n_down * rank, cw)
         partial[:, : n_down * rank] += lax.dot_general(
             hidden[:, cols(k)], weight, NT, preferred_element_type=jnp.float32
@@ -314,13 +316,13 @@
         return 0
 
     lax.fori_loop(0, parts, down_step, 0)
-    t = n - 1 + first_k
+    t = fill + first_k
     scatter_start(partial, rs_buf, rs_send, rs_recv)
-    relay_range(t, t + 2)
+    relay_range(t, t + 4)
     gather_start(
         scatter_wait(partial, rs_buf, rs_send, rs_recv), rank_low, ag_send, ag_recv
     )
-    relay_range(t + 2, t + 4)
+    relay_range(t + 4, t + 8)
     for copy in base_copies[1:]:
         copy.wait()
     gather_wait(rank_low, ag_send, ag_recv)
@@ -365,7 +367,7 @@
     low_q = low[:, :rank]
 
     def query_step(j, _):
-        relay(t + 4 + j)
+        relay(t + 8 + j)
         adapted_q = base_q[:, cols(j)].astype(jnp.float32) + jnp.dot(
             low_q, final[first_q + j], preferred_element_type=jnp.float32
         )
@@ -375,11 +377,11 @@
         return 0
 
     lax.fori_loop(0, parts, query_step, 0)
-    relay_range(t + 4 + parts, n - 1 + first_ou)
+    relay_range(t + 8 + parts, fill + first_ou)
     lax.fori_loop(1, n, kv_wait, 0)
 
     def head_step(j, _):
-        relay(n - 1 + first_ou + j)
+        relay(fill + first_ou + j)
         for h in range(heads_per_chunk):
             span = slice(h * HEAD_SIZE, (h + 1) * HEAD_SIZE)
             group = (j * heads_per_chunk + h) // group_size
@@ -468,7 +470,7 @@
     share = rows // tp
     smem = pl.BlockSpec(memory_space=pltpu.SMEM)
     vmem = pl.BlockSpec(memory_space=pltpu.VMEM)
-    hbm = pl.BlockSpec(memory_space=pl.ANY)
+    hbm = pl.BlockSpec(memory_space=pltpu.HBM)
     out = jax.ShapeDtypeStruct((rows, width), bf16)
     return pl.pallas_call(
         functools.partial(kernel, n, tp, width // kv_width),

time: 171 us -> 88.9 us (0.52)
  Pallas kernels: 158 us -> 75.1 us
    pallas_call x1, Pallas kernels: 158 us -> 75.1 us  [shards(): pl.pallas_call(functools.partial(kernel, n, tp, width // kv_width), out_s...]
where the time goes in v2:
time: 88.9 us; the launch traced here: 88.4 us
  Pallas kernels  75.1 us (84%)
  local copies, waits for them, and re-layouts  11.9 us (13%)
  between operations  1.31 us (1%)
    pallas_call x1, Pallas kernels, shards(): pl.pallas_call(functools.partial(kernel, n, tp, width // kv_width), out_s...  75.1 us
    unnamed x24, local copies, waits for them, and re-layouts  11.9 us

profile of v2, /device:TPU:0, one launch (start us, length us, event | category | flops | bytes accessed | tf_op | source)
XLA Modules:
  0.0 88.4 jit_solution(14377798696092322527)
XLA Ops:
  1.3 0.0 copy-start
  1.3 1.2 %copy-done = bf16[1,4,64,2048]{3,2,1,0:T(8,128)(2,1)S(1)} copy-done((bf16[1,4,64,2048]{3,2,1,0:T(8,128)(2,1)S(1)}, bf16[1,4,64,2048]{3,2,1,0:T(8,128)(2,1)}, u32[]{:S(2)}) %copy-start) | copy-done | bytes 1048600
  2.5 0.0 copy-start.1
  2.5 1.2 %copy-done.1 = bf16[1,4,64,2048]{3,2,1,0:T(8,128)(2,1)S(1)} copy-done((bf16[1,4,64,2048]{3,2,1,0:T(8,128)(2,1)S(1)}, bf16[1,4,64,2048]{3,2,1,0:T(8,128)(2,1)}, u32[]{:S(2)}) %copy-start.1) | copy-done | bytes 1048600
  3.7 0.0 copy-start.2
  3.7 1.2 %copy-done.2 = bf16[1,4,64,2048]{3,2,1,0:T(8,128)(2,1)S(1)} copy-done((bf16[1,4,64,2048]{3,2,1,0:T(8,128)(2,1)S(1)}, bf16[1,4,64,2048]{3,2,1,0:T(8,128)(2,1)}, u32[]{:S(2)}) %copy-start.2) | copy-done | bytes 1048600
  5.0 0.0 copy-start.3
  5.0 1.0 %copy-done.3 = bf16[128,2048]{1,0:T(8,128)(2,1)S(1)} copy-done((bf16[128,2048]{1,0:T(8,128)(2,1)S(1)}, bf16[128,2048]{1,0:T(8,128)(2,1)}, u32[]{:S(2)}) %copy-start.3) | copy-done | bytes 524312
  6.0 0.0 copy-start.4
  6.0 1.0 %copy-done.4 = bf16[128,2048]{1,0:T(8,128)(2,1)S(1)} copy-done((bf16[128,2048]{1,0:T(8,128)(2,1)S(1)}, bf16[128,2048]{1,0:T(8,128)(2,1)}, u32[]{:S(2)}) %copy-start.4) | copy-done | bytes 524312
  7.0 0.0 copy-start.5
  7.0 0.9 %copy-done.5 = bf16[1,4,2,64,256]{4,3,2,1,0:T(8,128)(2,1)S(1)} copy-done((bf16[1,4,2,64,256]{4,3,2,1,0:T(8,128)(2,1)S(1)}, bf16[1,4,2,64,256]{4,3,2,1,0:T(8,128)(2,1)}, u32[]{:S(2)}) %copy-start.5) | copy-done | bytes 262168
  8.0 0.0 copy-start.6
  8.0 0.8 copy-done.6
  8.8 0.0 copy-start.7
  8.8 0.8 copy-done.7
  9.7 0.0 copy-start.8
  9.7 0.7 copy-done.8
  10.3 0.0 copy-start.9
  10.3 0.7 copy-done.9
  11.0 0.0 copy-start.10
  11.0 0.7 copy-done.10
  11.6 75.1 %shard_map.140 = (bf16[128,2048]{1,0:T(8,128)(2,1)S(1)}, bf16[128,2048]{1,0:T(8,128)(2,1)S(1)}) custom-call(s32[8]{0:T(128)S(1)} %copy-done.8, s32[4]{0:T(128)S(1)} %copy-done.9, s32[1]{0:T(128)S(6)} %copy.17.publisher_ref, f32[1,128]{1,0:T(1,128)S(1)} %copy-done.10, bf16[128,2048]{1,0:T(8,128)(2,1)S(1)} %copy-done.3, bf16[128,2048]{1,0:T(8,128)(2,1)S(1)} %copy-done.4, ...), custom_call_target="tpu_custom_call" | custom-call | tf_op jit(solution)/shard_map/pallas_call | solution.py:475
  86.8 0.8 copy.18
  87.6 0.8 copy.19
Async XLA Ops:
  1.3 1.2 %copy-start = (bf16[1,4,64,2048]{3,2,1,0:T(8,128)(2,1)S(1)}, bf16[1,4,64,2048]{3,2,1,0:T(8,128)(2,1)}, u32[]{:S(2)}) copy-start(bf16[1,4,64,2048]{3,2,1,0:T(8,128)(2,1)} %up_q_hbm.1) | copy-start | bytes 3145732
  2.5 1.2 %copy-start.1 = (bf16[1,4,64,2048]{3,2,1,0:T(8,128)(2,1)S(1)}, bf16[1,4,64,2048]{3,2,1,0:T(8,128)(2,1)}, u32[]{:S(2)}) copy-start(bf16[1,4,64,2048]{3,2,1,0:T(8,128)(2,1)} %outer_down_hbm.1) | copy-start | bytes 3145732
  3.7 1.2 %copy-start.2 = (bf16[1,4,64,2048]{3,2,1,0:T(8,128)(2,1)S(1)}, bf16[1,4,64,2048]{3,2,1,0:T(8,128)(2,1)}, u32[]{:S(2)}) copy-start(bf16[1,4,64,2048]{3,2,1,0:T(8,128)(2,1)} %outer_up_hbm.1) | copy-start | bytes 3145732
  5.0 1.0 %copy-start.3 = (bf16[128,2048]{1,0:T(8,128)(2,1)S(1)}, bf16[128,2048]{1,0:T(8,128)(2,1)}, u32[]{:S(2)}) copy-start(bf16[128,2048]{1,0:T(8,128)(2,1)} %hidden_hbm.1) | copy-start | bytes 1572868
  6.0 1.0 %copy-start.4 = (bf16[128,2048]{1,0:T(8,128)(2,1)S(1)}, bf16[128,2048]{1,0:T(8,128)(2,1)}, u32[]{:S(2)}) copy-start(bf16[128,2048]{1,0:T(8,128)(2,1)} %base_q_hbm.1) | copy-start | bytes 1572868
  7.0 0.9 %copy-start.5 = (bf16[1,4,2,64,256]{4,3,2,1,0:T(8,128)(2,1)S(1)}, bf16[1,4,2,64,256]{4,3,2,1,0:T(8,128)(2,1)}, u32[]{:S(2)}) copy-start(bf16[1,4,2,64,256]{4,3,2,1,0:T(8,128)(2,1)} %up_kv_hbm.1) | copy-start | bytes 786436
  8.0 0.8 copy-start.6
  8.8 0.8 copy-start.7
  9.7 0.7 copy-start.8
  10.3 0.7 copy-start.9
  11.0 0.7 copy-start.10

commit v3 on v2

--- a/solution.py
+++ b/solution.py
@@ -11,6 +11,7 @@
 HEAD_SIZE = 128
 ADAPTER_RANK = 64
 NEG_BIG = -1e30
+SCALE = HEAD_SIZE**-0.5 * 1.4426950408889634
 NT = (((1,), (1,)), ((), ()))
 PARTS = 8
 LAG = 4
@@ -373,43 +374,56 @@
         )
         for h in range(heads_per_chunk):
             span = slice(h * HEAD_SIZE, (h + 1) * HEAD_SIZE)
-            queries[j, :, span] = rotate(adapted_q[:, span]).astype(jnp.bfloat16)
+            queries[j * heads_per_chunk + h] = rotate(adapted_q[:, span]).astype(jnp.bfloat16)
         return 0
 
     lax.fori_loop(0, parts, query_step, 0)
     relay_range(t + 8 + parts, fill + first_ou)
     lax.fori_loop(1, n, kv_wait, 0)
 
-    def head_step(j, _):
-        relay(fill + first_ou + j)
-        for h in range(heads_per_chunk):
-            span = slice(h * HEAD_SIZE, (h + 1) * HEAD_SIZE)
-            group = (j * heads_per_chunk + h) // group_size
-            key_block = kv_all[:, group].reshape(n * rows, HEAD_SIZE)
-            value_block = kv_all[:, groups + group].reshape(n * rows, HEAD_SIZE)
-            scores = (
-                lax.dot_general(
-                    queries[j, :, span], key_block, NT, preferred_element_type=jnp.float32
-                )
-                * HEAD_SIZE ** (-0.5)
-                + bias[...]
+    heads = width // HEAD_SIZE
+    batch = min(4, group_size)
+    batches = heads // batch
+    relays = -(-parts // batches)
+    chunks = batch // heads_per_chunk
+
+    def head_step(i, _):
+        for r in range(relays):
+            @pl.when(i * relays + r < parts)
+            def _():
+                relay(fill + first_ou + i * relays + r)
+
+        group = i * batch // group_size
+        key_block = kv_all[:, group].reshape(n * rows, HEAD_SIZE)
+        value_block = kv_all[:, groups + group].reshape(n * rows, HEAD_SIZE)
+        query_block = queries[pl.ds(i * batch, batch)].reshape(batch * rows, HEAD_SIZE)
+        scores = lax.dot_general(
+            query_block, key_block, NT, preferred_element_type=jnp.float32
+        ).reshape(batch, rows, n * rows)
+        scores = scores + bias[...][None]
+        raw = jnp.exp2((scores - jnp.max(scores, axis=2, keepdims=True)) * SCALE)
+        totals = jnp.sum(raw, axis=2, keepdims=True)
+        mixed = jnp.dot(
+            raw.astype(jnp.bfloat16).reshape(batch * rows, n * rows),
+            value_block,
+            preferred_element_type=jnp.float32,
+        ).reshape(batch, rows, HEAD_SIZE)
+        mixed = (mixed / totals).astype(jnp.bfloat16)
+        for h in range(batch):
+            place = pl.ds(pl.multiple_of((i * batch + h) * HEAD_SIZE, HEAD_SIZE), HEAD_SIZE)
+            attended_ref[:, place] = mixed[h]
+        added = jnp.zeros((rows, rank), jnp.float32)
+        for c in range(chunks):
+            added += lax.dot_general(
+                attended_ref[:, cols(i * chunks + c)],
+                final[first_od + i * chunks + c],
+                NT,
+                preferred_element_type=jnp.float32,
             )
-            raw = jnp.exp(scores - jnp.max(scores, axis=1, keepdims=True))
-            totals = jnp.sum(raw, axis=1, keepdims=True)
-            mixed = jnp.dot(
-                raw.astype(jnp.bfloat16), value_block, preferred_element_type=jnp.float32
-            )
-            place = pl.ds(pl.multiple_of(j * cw + h * HEAD_SIZE, HEAD_SIZE), HEAD_SIZE)
-            attended_ref[:, place] = (mixed / totals).astype(jnp.bfloat16)
-        partial2[:, :rank] += lax.dot_general(
-            attended_ref[:, cols(j)],
-            final[first_od + j],
-            NT,
-            preferred_element_type=jnp.float32,
-        )
-        return 0
-
-    lax.fori_loop(0, parts, head_step, 0)
+        partial2[:, :rank] += added
+        return 0
+
+    lax.fori_loop(0, batches, head_step, 0)
     scatter_start(partial2, rs_buf2, rs2_send, rs2_recv)
     gather_start(
         scatter_wait(partial2, rs_buf2, rs2_send, rs2_recv), out_low, ag2_send, ag2_recv
@@ -430,13 +444,10 @@
     gather_wait(out_low, ag2_send, ag2_recv)
     outer = out_low[:, :rank]
 
-    def up_step(j, _):
-        adapted_ref[:, cols(j)] = jnp.dot(
+    for j in range(parts):
+        adapted_ref[:, j * cw : (j + 1) * cw] = jnp.dot(
             outer, final[first_ou + j], preferred_element_type=jnp.float32
         ).astype(jnp.bfloat16)
-        return 0
-
-    lax.fori_loop(0, parts, up_step, 0)
 
 
 def shards(
@@ -488,7 +499,7 @@
             chunk,
             chunk,
             chunk,
-            pltpu.VMEM((PARTS, rows, cw), bf16),
+            pltpu.VMEM((width // HEAD_SIZE, rows, HEAD_SIZE), bf16),
             pltpu.VMEM((n, 2 * groups, rows, HEAD_SIZE), bf16),
             pltpu.VMEM((rows, n * rows), f32),
             pltpu.VMEM((rows, HEAD_SIZE), f32),
@@ -510,7 +521,7 @@
         ]
         + [dma((tp,))] * 8,
         compiler_params=pltpu.CompilerParams(
-            collective_id=0, has_side_effects=True, vmem_limit_bytes=48 * 1024 * 1024
+            collective_id=0, has_side_effects=True, vmem_limit_bytes=63 * 1024 * 1024
         ),
     )(
         stored_block_order,

time: 88.9 us -> 79.2 us (0.89)
  local copies, waits for them, and re-layouts: 11.9 us -> 3.76 us
  Pallas kernels: 75.1 us -> 74 us
    unnamed x24 -> x2, local copies, waits for them, and re-layouts: 11.9 us -> 3.76 us
    pallas_call x1, Pallas kernels: 75.1 us -> 74 us  [shards(): pl.pallas_call(functools.partial(kernel, n, tp, width // kv_width), out_s...]
where the time goes in v3:
time: 79.2 us; the launch traced here: 79 us
  Pallas kernels  74 us (93%)
  local copies, waits for them, and re-layouts  3.76 us (5%)
  between operations  1.29 us (2%)
    pallas_call x1, Pallas kernels, shards(): pl.pallas_call(functools.partial(kernel, n, tp, width // kv_width), out_s...  74 us
    unnamed x2, local copies, waits for them, and re-layouts  3.76 us

profile of v3, /device:TPU:0, one launch (start us, length us, event | category | flops | bytes accessed | tf_op | source)
XLA Modules:
  0.0 79.0 jit_solution(10338759974791569456)
XLA Ops:
  1.3 74.0 %shard_map.140 = (bf16[128,2048]{1,0:T(8,128)(2,1)}, bf16[128,2048]{1,0:T(8,128)(2,1)}) custom-call(s32[8]{0:T(128)} %order_ref.1, s32[4]{0:T(128)} %version_ref.1, s32[1]{0:T(128)S(6)} %copy.17.publisher_ref, f32[1,128]{1,0:T(1,128)} %constant.2.clone.frequency_ref, bf16[128,2048]{1,0:T(8,128)(2,1)} %hidden_hbm.1, bf16[128,2048]{1,0:T(8,128)(2,1)} %base_q_hbm.1, ...), custom_call_target="tpu_custom_call" | custom-call | tf_op jit(solution)/shard_map/pallas_call | solution.py:486
  75.2 1.9 %copy.18 = bf16[128,2048]{1,0:T(8,128)(2,1)} copy(bf16[128,2048]{1,0:T(8,128)(2,1)} %get-tuple-element.4) | data formatting | bytes 1048576
  77.1 1.9 %copy.19 = bf16[128,2048]{1,0:T(8,128)(2,1)} copy(bf16[128,2048]{1,0:T(8,128)(2,1)} %get-tuple-element.5) | data formatting | bytes 1048576
